TPU v7x, 512 devices: a whole 4x8x8 slice. The times are simulated.
512 devices in a mesh: row: 16 (over y, core), col: 32 (over z, x).
Axes of the slice: x: 4, y: 8, z: 8, core: 2. Of those that a mesh axis runs over, the one named last changes fastest.
Arguments:
- tokens: bfloat16 [256, 12288], P('col', 'row'), may hold values from -6 to 6
- up_weight: bfloat16 [12288, 24576], P('row', 'col'), may hold values from -0.0546875 to 0.0546875
- down_weight: bfloat16 [24576, 12288], P('col', 'row'), may hold values from -0.0390625 to 0.0390625
- cotangent: bfloat16 [256, 12288], P('col', 'row'), may hold values from -1.5 to 1.5
Outputs:
- layer_out: bfloat16 [256, 12288], P('col', 'row')
- input_grad: bfloat16 [256, 12288], P('col', 'row')
- up_grad: bfloat16 [12288, 24576], P('row', 'col')
- down_grad: bfloat16 [24576, 12288], P('col', 'row')
All inputs are finite; a program needn't handle non-finite values.
Results may differ from a plain program's by a relative error of at most 0.005.
Values may be sent and summed in bfloat16 or wider, within the bound.
A program may use at most 64 MiB of HBM per device.

v0:
```python
import math

import jax
import jax.numpy as jnp
from jax import lax
from jax.sharding import PartitionSpec as P

coeff_cubic = 0.044715
root_ratio = math.sqrt(2.0 / math.pi)


def gelu_parts(preact):
    inner = jnp.tanh(root_ratio * (preact + coeff_cubic * preact * preact * preact))
    values = 0.5 * preact * (1.0 + inner)
    slopes = 0.5 * (1.0 + inner) + 0.5 * preact * (1.0 - inner * inner) * root_ratio * (
        1.0 + 3.0 * coeff_cubic * preact * preact
    )
    return (values, slopes)


def contract_last(left, right):
    return lax.dot_general(
        left, right, (((1,), (1,)), ((), ())), preferred_element_type=jnp.float32
    )


def contract_first(left, right):
    return lax.dot_general(
        left, right, (((0,), (0,)), ((), ())), preferred_element_type=jnp.float32
    )


def local(tokens, up_weight, down_weight, cotangent):
    all_tokens, all_cotangent = (
        lax.all_gather(tokens, "col", axis=0, tiled=True),
        lax.all_gather(cotangent, "col", axis=0, tiled=True),
    )
    model_width = up_weight.shape[0]
    hidden_width = up_weight.shape[1]
    token_rows = all_tokens
    cotan_rows = all_cotangent
    forward_part = jnp.dot(token_rows, up_weight, preferred_element_type=jnp.float32)
    backward_part = contract_last(cotan_rows, down_weight)
    shares = lax.psum_scatter(
        jnp.concatenate([forward_part, backward_part], axis=1),
        "row",
        scatter_dimension=0,
        tiled=True,
    )
    values, slopes = gelu_parts(shares[:, :hidden_width])
    activated = values.astype(jnp.bfloat16)
    hidden_grad = (shares[:, hidden_width:] * slopes).astype(jnp.bfloat16)
    stacked = jnp.stack([activated, hidden_grad])
    segment = lax.all_gather(stacked, "row", axis=1, tiled=True)
    part_act = segment[0]
    part_grad = segment[1]
    token_rows = all_tokens
    cotan_rows = all_cotangent
    products = jnp.concatenate(
        [
            jnp.dot(part_act, down_weight, preferred_element_type=jnp.float32),
            contract_last(part_grad, up_weight),
        ],
        axis=1,
    )
    up_total = contract_first(token_rows, part_grad)
    down_total = contract_first(part_act, cotan_rows)
    results = lax.psum_scatter(products, "col", scatter_dimension=0, tiled=True)
    layer_out = results[:, :model_width].astype(jnp.bfloat16)
    input_grad = results[:, model_width:].astype(jnp.bfloat16)
    return (layer_out, input_grad, up_total.astype(jnp.bfloat16), down_total.astype(jnp.bfloat16))


def solution(mesh):
    in_specs = (P("col", "row"), P("row", "col"), P("col", "row"), P("col", "row"))
    out_specs = (P("col", "row"), P("col", "row"), P("row", "col"), P("col", "row"))
    return jax.shard_map(local, mesh=mesh, in_specs=in_specs, out_specs=out_specs, check_vma=False)
```

profile of v0, /device:TPU:1, one launch (start us, length us, event | category | flops | bytes accessed | tf_op | source)
XLA Modules:
  0.0 418.0 jit_solution(12255555794970134319)
XLA Ops:
  7.2 0.0 copy-start
  7.2 0.0 reduce-scatter.3.cloned.1.call-start
  7.2 44.5 %all_gather.9 = bf16[256,768]{1,0:T(8,128)(2,1)S(1)} all-gather(bf16[8,768]{1,0:T(8,128)(2,1)} %param.4), channel_id=1, replica_groups=mesh['row'=16,'col'=32] {'col'}, dimensions={0}, use_global_device_ids=true | all-gather | bytes 405504 | tf_op jit(solution)/shard_map/all_gather | solution.py:35
  51.7 0.0 copy-start.2
  51.7 36.0 %all_gather.10 = bf16[256,768]{1,0:T(8,128)(2,1)S(1)} all-gather(bf16[8,768]{1,0:T(8,128)(2,1)} %param.7), channel_id=1, replica_groups=mesh['row'=16,'col'=32] {'col'}, dimensions={0}, use_global_device_ids=true | all-gather | bytes 405504 | tf_op jit(solution)/shard_map/all_gather | solution.py:36
  87.8 0.0 copy-done.2
  87.8 1.8 fusion.13
  89.5 0.0 copy-done
  89.6 0.5 fusion.14
  90.1 1.3 pad_maximum_fusion
  91.4 0.0 reduce-scatter.3.cloned.1.call-update
  91.4 0.0 reduce-scatter.5.cloned.1.call-start
  91.5 79.3 %reduce-scatter.3.cloned.1.call-done = f32[16,1536]{1,0:T(8,128)} async-done(((f32[256,1536]{1,0:T(8,128)}), f32[16,1536]{1,0:T(8,128)}) %reduce-scatter.3.cloned.1.call-update) | async-done | bytes 98320 | tf_op jit(solution)/shard_map/reduce_scatter | solution.py:44
  170.8 0.9 fusion.10
  171.7 18.9 %all_gather.11 = bf16[2,256,768]{2,1,0:T(8,128)(2,1)S(1)} all-gather(bf16[2,16,768]{2,1,0:T(8,128)(2,1)S(1)} %pad_maximum_fusion.2), channel_id=1, replica_groups=mesh['row'=16,'col'=32] {'row'}, dimensions={1}, use_global_device_ids=true | all-gather | bytes 835584 | tf_op jit(solution)/shard_map/all_gather | solution.py:54
  190.6 0.0 copy-start.1
  190.6 0.5 fusion.1
  191.1 0.8 copy-done.1
  191.9 0.5 fusion.2
  192.4 1.3 pad_maximum_fusion.1
  193.7 0.0 reduce-scatter.5.cloned.1.call-update
  193.8 1.5 fusion
  195.3 1.5 copy.8
  196.7 1.5 convolution_convert_fusion
  198.3 211.5 %reduce-scatter.5.cloned.1.call-done = f32[8,1536]{1,0:T(8,128)} async-done(((f32[256,1536]{1,0:T(8,128)}), f32[8,1536]{1,0:T(8,128)}) %reduce-scatter.5.cloned.1.call-update) | async-done | bytes 49168 | tf_op jit(solution)/shard_map/reduce_scatter | solution.py:68
  409.7 0.8 convert.4
  410.5 0.6 fusion.12
  (1 shorter events, 0.0 us)
Async XLA Ops:
  7.2 82.4 %copy-start = (bf16[768,768]{1,0:T(8,128)(2,1)S(1)}, bf16[768,768]{1,0:T(8,128)(2,1)}, u32[]{:S(2)}) copy-start(bf16[768,768]{1,0:T(8,128)(2,1)} %param.6) | copy-start | bytes 3538948
  7.2 163.6 %reduce-scatter.3.cloned.1.call-start = ((), (), s32[]{:S(2)}) async-start(), calls=%async_computation.2 | async-start | bytes 1671168 | tf_op jit(solution)/shard_map/reduce_scatter | solution.py:44
  51.7 36.0 %copy-start.2 = (bf16[256,768]{1,0:T(8,128)(2,1)}, bf16[256,768]{1,0:T(8,128)(2,1)S(1)}, u32[]{:S(2)}) copy-start(bf16[256,768]{1,0:T(8,128)(2,1)S(1)} %all_gather.9) | copy-start | bytes 1179652
  91.4 318.3 %reduce-scatter.5.cloned.1.call-start = ((), (), s32[]{:S(2)}) async-start(), calls=%async_computation.3 | async-start | bytes 1622016 | tf_op jit(solution)/shard_map/reduce_scatter | solution.py:68
  190.6 1.3 copy-start.1
Sparse Core Ops, SparseCore 0:
  91.6 79.2 reduce-scatter.2
  193.9 215.7 reduce-scatter.4
where the time goes:
time: 423 us; the launch traced here: 418 us
  waiting for transfers between devices  291 us (69%)
  blocking collectives  99.5 us (24%)
  between operations  14.1 us (3%)
  matrix products  6.27 us (1%)
  other arithmetic  4.35 us (1%)
    reduce_scatter x1, waiting for transfers between devices, local(): results = lax.psum_scatter(products, 'col', scatter_dimension=0, tiled=True)  211 us
    reduce_scatter x1, waiting for transfers between devices, local(): lax.psum_scatter(jnp.concatenate([forward_part, backward_part], axis=1),...  79.3 us
    all_gather x1, blocking collectives, local(): lax.all_gather(tokens, 'col', axis=0, tiled=True)  44.5 us
    all_gather x1, blocking collectives, local(): lax.all_gather(cotangent, 'col', axis=0, tiled=True)  36 us
    all_gather x1, blocking collectives, local(): segment = lax.all_gather(stacked, 'row', axis=1, tiled=True)  18.9 us
  transfers between devices with their start and end apart: 2, of which 2 were waited for; matrix products, arithmetic and copies ran while one was open for 1% of the time, Pallas kernels for 0%

commit v1 on v0

v1 whole, which is shorter than its diff:
```python
import math

import jax
import jax.numpy as jnp
from jax import lax
from jax.experimental import pallas as pl
from jax.experimental.pallas import tpu as pltpu
from jax.sharding import PartitionSpec as P

coeff_cubic = 0.044715
root_ratio = math.sqrt(2.0 / math.pi)
MESH = pl.DeviceIdType.MESH
BF = jnp.bfloat16
F32 = jnp.float32

NY, NK, NZ, NX = 8, 2, 8, 4
NEAR = (1, 7, 2, 6, 3, 5, 4)
FAR = (4, 3, 5, 2, 6, 1, 7)


def gelu_parts(preact):
    inner = jnp.tanh(root_ratio * (preact + coeff_cubic * preact * preact * preact))
    values = 0.5 * preact * (1.0 + inner)
    slopes = 0.5 * (1.0 + inner) + 0.5 * preact * (1.0 - inner * inner) * root_ratio * (
        1.0 + 3.0 * coeff_cubic * preact * preact
    )
    return (values, slopes)


def dot(left, right, dims):
    return lax.dot_general(left, right, (dims, ((), ())), preferred_element_type=F32)


NN = ((1,), (0,))
NT = ((1,), (1,))
TN = ((0,), (0,))


def kernel(
    tok_ref, cot_ref, up_hbm, down_hbm,
    lo_ref, ig_ref, ug_hbm, dg_hbm,
    up, down, ug, dg,
    gat, xs, cs,
    part, pair, send_b, recv_b,
    ah, prod, send_x, recv_x, send_z, recv_z,
    wsem, gsem,
    az_s, ax_s, a_r,
    p_s, p_r,
    b_s, b_r,
    c_s, cf_s, c_r,
    dx_s, dx_r, dz_s, dz_r,
):
    w = up.shape[0]
    h = up.shape[1]
    row = lax.axis_index("row")
    col = lax.axis_index("col")
    y, k = row // NK, row % NK
    z, x = col // NX, col % NX

    def at_y(d):
        return (lax.rem(y + d, NY) * NK + k, col)

    def at_z(d):
        return (row, lax.rem(z + d, NZ) * NX + x)

    def at_x(d):
        return (row, z * NX + lax.rem(x + d, NX))

    other = (y * NK + 1 - k, col)

    def copy(src, dst, ss, rs, device):
        return pltpu.make_async_remote_copy(
            src_ref=src, dst_ref=dst, send_sem=ss, recv_sem=rs, device_id=device, device_id_type=MESH
        )

    load_up = pltpu.make_async_copy(up_hbm, up, wsem.at[0])
    load_down = pltpu.make_async_copy(down_hbm, down, wsem.at[1])
    load_up.start()
    load_down.start()

    barrier = pltpu.get_barrier_semaphore()
    peers = [at_y(d) for d in FAR] + [at_z(d) for d in FAR] + [at_x(d) for d in (2, 1, 3)] + [other]
    for device in peers:
        pl.semaphore_signal(barrier, inc=1, device_id=device, device_id_type=MESH)
    gat[col] = jnp.concatenate([tok_ref[...].astype(F32), cot_ref[...].astype(F32)], axis=0).astype(BF)
    pl.semaphore_wait(barrier, len(peers))

    pending = []
    for d in FAR:
        c = copy(gat.at[col], gat.at[col], az_s.at[d], a_r.at[col], at_z(d))
        c.start()
        pending.append(c)
    for s in (0,) + NEAR:
        slot = lax.rem(z + s, NZ) * NX + x
        if s:
            copy(gat.at[slot], gat.at[slot], az_s.at[0], a_r.at[slot], at_z(s)).wait_recv()
        for d in (2, 1, 3):
            c = copy(gat.at[slot], gat.at[slot], ax_s.at[s * NX + d], a_r.at[slot], at_x(d))
            c.start()
            pending.append(c)
    for s in (0,) + NEAR:
        zz = lax.rem(z + s, NZ)
        for d in (1, 3, 2):
            slot = zz * NX + lax.rem(x + d, NX)
            copy(gat.at[slot], gat.at[slot], az_s.at[0], a_r.at[slot], at_x(d)).wait_recv()
        blocks = [gat[zz * NX + i].astype(F32) for i in range(NX)]
        rows = pl.ds(pl.multiple_of(zz * 32, 32), 32)
        xs[rows, :] = jnp.concatenate([b[:8] for b in blocks], axis=0).astype(BF)
        cs[rows, :] = jnp.concatenate([b[8:] for b in blocks], axis=0).astype(BF)
    for c in pending:
        c.wait_send()

    load_up.wait()
    load_down.wait()
    part[:, :h] = dot(xs[...], up[...], NN)
    part[:, h:] = dot(cs[...], down[...], NT)

    mine = pl.ds(pl.multiple_of(k * 128, 128), 128)
    theirs = pl.ds(pl.multiple_of((1 - k) * 128, 128), 128)
    c = copy(part.at[theirs], pair, p_s, p_r, other)
    c.start()
    c.wait()
    pair[...] = pair[...] + part[mine, :]
    for b in range(NY):
        send_b[b] = pair[pl.ds(b * 16, 16), :].astype(BF)
    pending = []
    for d in FAR:
        to = lax.rem(y + d, NY)
        c = copy(send_b.at[to], recv_b.at[y], b_s.at[d], b_r.at[y], at_y(d))
        c.start()
        pending.append(c)
    total = pair[pl.ds(pl.multiple_of(y * 16, 16), 16), :]
    for s in NEAR:
        slot = lax.rem(y + s, NY)
        copy(recv_b.at[slot], recv_b.at[slot], b_s.at[0], b_r.at[slot], at_y(s)).wait_recv()
        total = total + recv_b[slot].astype(F32)
    for c in pending:
        c.wait_send()

    values, slopes = gelu_parts(total[:, :h])
    own = k * NY + y
    ah[own] = jnp.concatenate([values, total[:, h:] * slopes], axis=1).astype(BF)

    pending = []
    for d in FAR:
        c = copy(ah.at[own], ah.at[own], c_s.at[d], c_r.at[own], at_y(d))
        c.start()
        pending.append(c)
    for s in (0,) + NEAR:
        slot = k * NY + lax.rem(y + s, NY)
        if s:
            copy(ah.at[slot], ah.at[slot], c_s.at[0], c_r.at[slot], at_y(s)).wait_recv()
        c = copy(ah.at[slot], ah.at[slot], cf_s.at[s], c_r.at[slot], other)
        c.start()
        pending.append(c)
    for s in (0,) + NEAR:
        slot = (1 - k) * NY + lax.rem(y + s, NY)
        copy(ah.at[slot], ah.at[slot], c_s.at[0], c_r.at[slot], other).wait_recv()
    for c in pending:
        c.wait_send()

    prod[:, :w] = dot(ah[:, :, :h].reshape(256, h), down[...], NN)
    prod[:, w:] = dot(ah[:, :, h:].reshape(256, h), up[...], NT)

    pending = []
    for d in FAR + (0,):
        zz = lax.rem(z + d, NZ)
        for e in (2, 1, 3):
            to = lax.rem(x + e, NX)
            rows = pl.ds(pl.multiple_of(zz * 32 + to * 8, 8), 8)
            send_x[zz * NX + to] = jnp.concatenate([prod[rows, :w], prod[rows, w:]], axis=0).astype(BF)
            c = copy(
                send_x.at[zz * NX + to], recv_x.at[zz * NX + x],
                dx_s.at[d * NX + e], dx_r.at[zz * NX + x], at_x(e),
            )
            c.start()
            pending.append(c)

    ug[...] = dot(xs[...], ah[:, :, h:].reshape(256, h), TN).astype(BF)
    store_up = pltpu.make_async_copy(ug, ug_hbm, gsem.at[0])
    store_up.start()
    dg[...] = dot(ah[:, :, :h].reshape(256, h), cs[...], TN).astype(BF)
    store_down = pltpu.make_async_copy(dg, dg_hbm, gsem.at[1])
    store_down.start()

    for d in FAR + (0,):
        zz = lax.rem(z + d, NZ)
        rows = pl.ds(pl.multiple_of(zz * 32 + x * 8, 8), 8)
        total = jnp.concatenate([prod[rows, :w], prod[rows, w:]], axis=0)
        for e in (1, 3, 2):
            slot = zz * NX + lax.rem(x + e, NX)
            copy(recv_x.at[slot], recv_x.at[slot], dx_s.at[0], dx_r.at[slot], at_x(e)).wait_recv()
            total = total + recv_x[slot].astype(F32)
        if d:
            send_z[zz] = total.astype(BF)
            c = copy(send_z.at[zz], recv_z.at[z], dz_s.at[d], dz_r.at[z], at_z(d))
            c.start()
            pending.append(c)
    for s in NEAR:
        slot = lax.rem(z + s, NZ)
        copy(recv_z.at[slot], recv_z.at[slot], dz_s.at[0], dz_r.at[slot], at_z(s)).wait_recv()
        total = total + recv_z[slot].astype(F32)
    lo_ref[...] = total[:8].astype(BF)
    ig_ref[...] = total[8:].astype(BF)
    for c in pending:
        c.wait_send()
    store_up.wait()
    store_down.wait()


def local(tokens, up_weight, down_weight, cotangent):
    w, h = up_weight.shape
    dma = pltpu.SemaphoreType.DMA
    vmem = pl.BlockSpec(memory_space=pltpu.VMEM)
    hbm = pl.BlockSpec(memory_space=pl.ANY)
    lo, ig, ug, dg = pl.pallas_call(
        kernel,
        out_shape=(
            jax.ShapeDtypeStruct((8, w), BF),
            jax.ShapeDtypeStruct((8, w), BF),
            jax.ShapeDtypeStruct((w, h), BF),
            jax.ShapeDtypeStruct((h, w), BF),
        ),
        in_specs=[vmem, vmem, hbm, hbm],
        out_specs=(vmem, vmem, hbm, hbm),
        scratch_shapes=[
            pltpu.VMEM((w, h), BF), pltpu.VMEM((h, w), BF), pltpu.VMEM((w, h), BF), pltpu.VMEM((h, w), BF),
            pltpu.VMEM((32, 16, w), BF), pltpu.VMEM((256, w), BF), pltpu.VMEM((256, w), BF),
            pltpu.VMEM((256, 2 * h), F32), pltpu.VMEM((128, 2 * h), F32),
            pltpu.VMEM((NY, 16, 2 * h), BF), pltpu.VMEM((NY, 16, 2 * h), BF),
            pltpu.VMEM((16, 16, 2 * h), BF), pltpu.VMEM((256, 2 * w), F32),
            pltpu.VMEM((32, 16, w), BF), pltpu.VMEM((32, 16, w), BF),
            pltpu.VMEM((NZ, 16, w), BF), pltpu.VMEM((NZ, 16, w), BF),
            dma((2,)), dma((2,)),
            dma((NZ,)), dma((NZ * NX,)), dma((NZ * NX,)),
            dma, dma,
            dma((NY,)), dma((NY,)),
            dma((NY,)), dma((NY,)), dma((2 * NY,)),
            dma((NZ * NX,)), dma((NZ * NX,)), dma((NZ,)), dma((NZ,)),
        ],
        compiler_params=pltpu.CompilerParams(
            collective_id=0, has_side_effects=True, vmem_limit_bytes=48 << 20
        ),
        cost_estimate=pl.CostEstimate(flops=1812000000, bytes_accessed=4800000, transcendentals=12288),
        name="sublayer",
    )(tokens, cotangent, up_weight, down_weight)
    return lo, ig, ug, dg


def solution(mesh):
    in_specs = (P("col", "row"), P("row", "col"), P("col", "row"), P("col", "row"))
    out_specs = (P("col", "row"), P("col", "row"), P("row", "col"), P("col", "row"))
    return jax.shard_map(local, mesh=mesh, in_specs=in_specs, out_specs=out_specs, check_vma=False)
```

time: 423 us -> 78.7 us (0.19); the launches traced: 418 us -> 78.4 us
  waiting for transfers between devices: 291 us -> 0 us
  blocking collectives: 99.5 us -> 0 us
  Pallas kernels: 0 us -> 70.6 us
  between operations: 14.1 us -> 0.65 us
  matrix products: 6.27 us -> 0 us
  other arithmetic: 4.35 us -> 0 us
  local copies, waits for them, and re-layouts: 2.86 us -> 7.17 us
    reduce_scatter x2 -> x0, waiting for transfers between devices: 291 us -> none  [the longest x1 211 us: local(): results = lax.psum_scatter(products, 'col', scatter_dimension=0, tiled=True)]
    all_gather x3 -> x0, blocking collectives: 99.5 us -> none  [the longest x1 44.5 us: local(): lax.all_gather(tokens, 'col', axis=0, tiled=True)]
    pallas_call x0 -> x1, Pallas kernels: none -> 70.6 us  [local(): pl.pallas_call(kernel, out_shape=(jax.ShapeDtypeStruct((8, w), BF), jax.S...]
    dot_general x6 -> x0, matrix products: 6.27 us -> none  [the longest x2 3.04 us: contract_first(): lax.dot_general(left, right, (((0,), (0,)), ((), ())), preferred_element_...]
    unnamed x7 -> x12, local copies, waits for them, and re-layouts: 2.25 us -> 7.17 us
  transfers between devices with their start and end apart: 2 -> 0, of which waited for: 2 -> 0; matrix products, arithmetic and copies ran while one was open for 1% -> 0% of each run, Pallas kernels for 0% -> 0%
where the time goes in v1:
time: 78.7 us; the launch traced here: 78.4 us
  Pallas kernels  70.6 us (90%)
  local copies, waits for them, and re-layouts  7.17 us (9%)
    pallas_call x1, Pallas kernels, local(): pl.pallas_call(kernel, out_shape=(jax.ShapeDtypeStruct((8, w), BF), jax.S...  70.6 us
    unnamed x12, local copies, waits for them, and re-layouts  7.17 us

profile of v1, /device:TPU:1, one launch (start us, length us, event | category | flops | bytes accessed | tf_op | source)
XLA Modules:
  0.0 78.4 jit_solution(6583702358743987789)
XLA Ops:
  0.6 0.0 copy-start
  0.6 1.3 %copy-done = bf16[768,768]{1,0:T(8,128)(2,1)S(1)} copy-done((bf16[768,768]{1,0:T(8,128)(2,1)S(1)}, bf16[768,768]{1,0:T(8,128)(2,1)}, u32[]{:S(2)}) %copy-start) | copy-done | bytes 1179672
  1.9 0.0 copy-start.1
  1.9 1.3 %copy-done.1 = bf16[768,768]{1,0:T(8,128)(2,1)S(1)} copy-done((bf16[768,768]{1,0:T(8,128)(2,1)S(1)}, bf16[768,768]{1,0:T(8,128)(2,1)}, u32[]{:S(2)}) %copy-start.1) | copy-done | bytes 1179672
  3.2 0.0 copy-start.2
  3.2 0.7 copy-done.2
  3.9 0.0 copy-start.3
  3.9 0.7 copy-done.3
  4.6 70.6 %sublayer.1 = (bf16[8,768]{1,0:T(8,128)(2,1)S(1)}, bf16[8,768]{1,0:T(8,128)(2,1)S(1)}, bf16[768,768]{1,0:T(8,128)(2,1)S(1)}, bf16[768,768]{1,0:T(8,128)(2,1)S(1)}) custom-call(bf16[8,768]{1,0:T(8,128)(2,1)S(1)} %copy-done.2, bf16[8,768]{1,0:T(8,128)(2,1)S(1)} %copy-done.3, bf16[768,768]{1,0:T(8,128)(2,1)S(1)} %copy-done, bf16[768,768]{1,0:T(8,128)(2,1)S(1)} %copy-done.1), custom_call_target="tpu_custom_call" | custom-call | flops 1812000000 | bytes 4800000 | tf_op jit(solution)/shard_map/sublayer/pallas_call | solution.py:216
  75.2 0.6 copy.12
  75.8 0.6 copy.13
  76.4 1.0 %copy.14 = bf16[768,768]{1,0:T(8,128)(2,1)} copy(bf16[768,768]{1,0:T(8,128)(2,1)S(1)} %get-tuple-element.10) | data formatting | bytes 2359296
  77.4 1.0 %copy.15 = bf16[768,768]{1,0:T(8,128)(2,1)} copy(bf16[768,768]{1,0:T(8,128)(2,1)S(1)} %get-tuple-element.11) | data formatting | bytes 2359296
Async XLA Ops:
  0.6 1.3 %copy-start = (bf16[768,768]{1,0:T(8,128)(2,1)S(1)}, bf16[768,768]{1,0:T(8,128)(2,1)}, u32[]{:S(2)}) copy-start(bf16[768,768]{1,0:T(8,128)(2,1)} %up_hbm.1) | copy-start | bytes 3538948
  1.9 1.3 %copy-start.1 = (bf16[768,768]{1,0:T(8,128)(2,1)S(1)}, bf16[768,768]{1,0:T(8,128)(2,1)}, u32[]{:S(2)}) copy-start(bf16[768,768]{1,0:T(8,128)(2,1)} %down_hbm.1) | copy-start | bytes 3538948
  3.2 0.7 copy-start.2
  3.9 0.7 copy-start.3

commit v2 on v0

v2 whole, which is shorter than its diff:
```python
import math

import jax
import jax.numpy as jnp
from jax import lax
from jax.experimental import pallas as pl
from jax.experimental.pallas import tpu as pltpu
from jax.sharding import PartitionSpec as P

coeff_cubic = 0.044715
root_ratio = math.sqrt(2.0 / math.pi)
MESH = pl.DeviceIdType.MESH
BF = jnp.bfloat16
F32 = jnp.float32

NY, NK, NZ, NX = 8, 2, 8, 4
NEAR = (1, 7, 2, 6, 3, 5, 4)
FAR = (4, 3, 5, 2, 6, 1, 7)


def gelu_parts(preact):
    inner = jnp.tanh(root_ratio * (preact + coeff_cubic * preact * preact * preact))
    values = 0.5 * preact * (1.0 + inner)
    slopes = 0.5 * (1.0 + inner) + 0.5 * preact * (1.0 - inner * inner) * root_ratio * (
        1.0 + 3.0 * coeff_cubic * preact * preact
    )
    return (values, slopes)


def dot(left, right, dims):
    return lax.dot_general(left, right, (dims, ((), ())), preferred_element_type=F32)


NN = ((1,), (0,))
NT = ((1,), (1,))
TN = ((0,), (0,))


def fold(block):
    half = block.shape[1] // 2
    return jnp.concatenate([block[:, :half], block[:, half:]], axis=0)


def unfold(block):
    return jnp.concatenate([block[:8], block[8:]], axis=1)


def kernel(
    tok_hbm, cot_hbm, up_hbm, down_hbm,
    lo_ref, ig_ref, ug_ref, dg_ref,
    up, down, shard, gat, xs, part, pair, send_b, recv_b, ah, prod, send_x, recv_x, send_z, recv_z,
    wsem, az_s, az_r, ax_s, ax_r, p_s, p_r, b_s, b_r, c_s, c_r, f_s, f_r, dx_s, dx_r, dz_s, dz_r,
):
    row = lax.axis_index("row")
    col = lax.axis_index("col")
    y, k = row // NK, row % NK
    z, x = col // NX, col % NX

    def at_y(d):
        return (lax.rem(y + d, NY) * NK + k, col)

    def at_z(d):
        return (row, lax.rem(z + d, NZ) * NX + x)

    def at_x(d):
        return (row, z * NX + lax.rem(x + d, NX))

    other = (y * NK + 1 - k, col)
    pending = []

    def copy(src, dst, ss, rs, device):
        return pltpu.make_async_remote_copy(
            src_ref=src, dst_ref=dst, send_sem=ss, recv_sem=rs, device_id=device, device_id_type=MESH
        )

    def send(src, dst, ss, rs, device):
        c = copy(src, dst, ss, rs, device)
        c.start()
        pending.append(c)

    def arrived(dst, ss, rs, device):
        copy(dst, dst, ss, rs, device).wait_recv()

    load_tok = pltpu.make_async_copy(tok_hbm, shard.at[0], wsem.at[0])
    load_cot = pltpu.make_async_copy(cot_hbm, shard.at[1], wsem.at[1])
    load_up = pltpu.make_async_copy(up_hbm, up, wsem.at[2])
    load_down = pltpu.make_async_copy(down_hbm, down, wsem.at[3])
    load_tok.start()
    load_cot.start()
    load_up.start()
    load_down.start()

    barrier = pltpu.get_barrier_semaphore()
    peers = [at_y(d) for d in FAR] + [at_z(d) for d in FAR] + [at_x(d) for d in (2, 1, 3)] + [other]
    for device in peers:
        pl.semaphore_signal(barrier, inc=1, device_id=device, device_id_type=MESH)
    load_tok.wait()
    load_cot.wait()
    for n in (0, 1):
        gat[n, x, z] = fold(shard[n].astype(F32)).astype(BF)
    pl.semaphore_wait(barrier, len(peers))

    for n in (0, 1):
        for d in FAR:
            send(gat.at[n, x, z], gat.at[n, x, z], az_s.at[n, d], az_r.at[n, z], at_z(d))
    for n in (0, 1):
        for s in (0, 1, 3, 2):
            p = lax.rem(z // 2 + s, NZ // 2)
            if s == 0:
                mate = z + 1 - 2 * lax.rem(z, 2)
                arrived(gat.at[n, x, mate], az_s.at[n, 0], az_r.at[n, mate], at_z(1))
            else:
                for i in (0, 1):
                    arrived(gat.at[n, x, 2 * p + i], az_s.at[n, 0], az_r.at[n, 2 * p + i], at_z(1))
            for d in (2, 1, 3):
                block = gat.at[n, x, pl.ds(2 * p, 2)]
                send(block, block, ax_s.at[n, s, d], ax_r.at[n, x, p], at_x(d))
    for n in (0, 1):
        for s in (0, 1, 3, 2):
            p = lax.rem(z // 2 + s, NZ // 2)
            for d in (1, 3, 2):
                xx = lax.rem(x + d, NX)
                arrived(gat.at[n, xx, pl.ds(2 * p, 2)], ax_s.at[n, 0, 0], ax_r.at[n, xx, p], at_x(d))
            blocks = [unfold(gat[n, j, 2 * p + i].astype(F32)) for i in (0, 1) for j in range(NX)]
            xs[n, pl.ds(pl.multiple_of(p * 64, 64), 64), :] = jnp.concatenate(blocks, axis=0).astype(BF)

        mine = pl.ds(pl.multiple_of(k * 128, 128), 128)
        theirs = pl.ds(pl.multiple_of((1 - k) * 128, 128), 128)
        if n == 0:
            load_up.wait()
        else:
            load_down.wait()
        weight, dims = ((up, NN), (down, NT))[n]
        part[n, 0] = dot(xs[n, theirs, :], weight[...], dims)
        send(part.at[n, 0], pair.at[n], p_s.at[n], p_r.at[n], other)
        part[n, 1] = dot(xs[n, mine, :], weight[...], dims)

    for n in (0, 1):
        arrived(pair.at[n], p_s.at[n], p_r.at[n], other)
        for d in FAR + (0,):
            to = lax.rem(y + d, NY)
            rows = pl.ds(pl.multiple_of(to * 16, 16), 16)
            total = part[n, 1, rows, :] + pair[n, rows, :]
            if d:
                send_b[n, to] = total.astype(BF)
                send(send_b.at[n, to], recv_b.at[n, y], b_s.at[n, d], b_r.at[n, y], at_y(d))
            else:
                part[n, 1, rows, :] = total
    own = pl.ds(pl.multiple_of(y * 16, 16), 16)
    at = k * NY + y
    for n in (0, 1):
        total = part[n, 1, own, :]
        for s in NEAR:
            slot = lax.rem(y + s, NY)
            arrived(recv_b.at[n, slot], b_s.at[n, 0], b_r.at[n, slot], at_y(s))
            total = total + recv_b[n, slot].astype(F32)
        if n == 0:
            values, slopes = gelu_parts(total)
            ah[0, at] = values.astype(BF)
        else:
            ah[1, at] = (total * slopes).astype(BF)
        for d in FAR:
            send(ah.at[n, at], ah.at[n, at], c_s.at[n, d], c_r.at[n, y], at_y(d))
        send(ah.at[n, at], ah.at[n, at], f_s.at[n, 0], f_r.at[n, y], other)
    for n in (0, 1):
        for s in NEAR:
            yy = lax.rem(y + s, NY)
            block = ah.at[n, k * NY + yy]
            arrived(block, c_s.at[n, 0], c_r.at[n, yy], at_y(s))
            send(block, block, f_s.at[n, s], f_r.at[n, yy], other)
        for s in (0,) + NEAR:
            yy = lax.rem(y + s, NY)
            arrived(ah.at[n, (1 - k) * NY + yy], f_s.at[n, 0], f_r.at[n, yy], other)
        weight, dims = ((down, NN), (up, NT))[n]
        prod[n] = dot(ah[n].reshape(256, ah.shape[3]), weight[...], dims)
        for s in (2, 1, 3, 0):
            p = lax.rem(z // 2 + s, NZ // 2)
            for e in (2, 1, 3):
                to = lax.rem(x + e, NX)
                for i in (0, 1):
                    rows = pl.ds(pl.multiple_of(p * 64 + i * 32 + to * 8, 8), 8)
                    send_x[n, to, 2 * p + i] = fold(prod[n, rows, :]).astype(BF)
                send(
                    send_x.at[n, to, pl.ds(2 * p, 2)], recv_x.at[n, x, pl.ds(2 * p, 2)],
                    dx_s.at[n, s, e], dx_r.at[n, x, p], at_x(e),
                )

    totals = []
    for n in (0, 1):
        for s in (2, 1, 3, 0):
            p = lax.rem(z // 2 + s, NZ // 2)
            for e in (1, 3, 2):
                xx = lax.rem(x + e, NX)
                arrived(recv_x.at[n, xx, pl.ds(2 * p, 2)], dx_s.at[n, 0, 0], dx_r.at[n, xx, p], at_x(e))
            for i in (0, 1):
                zz = 2 * p + i if s else (z + 1 - 2 * lax.rem(z, 2), z)[i]
                rows = pl.ds(pl.multiple_of(zz * 32 + x * 8, 8), 8)
                total = fold(prod[n, rows, :])
                for e in (1, 3, 2):
                    total = total + recv_x[n, lax.rem(x + e, NX), zz].astype(F32)
                if s or i == 0:
                    send_z[n, zz] = total.astype(BF)
                    send(send_z.at[n, zz], recv_z.at[n, z], dz_s.at[n, 2 * s + i], dz_r.at[n, z], (row, zz * NX + x))
        totals.append(total)
        if n == 0:
            ug_ref[...] = dot(xs[0], ah[1].reshape(256, ah.shape[3]), TN).astype(BF)
            dg_ref[...] = dot(ah[0].reshape(256, ah.shape[3]), xs[1], TN).astype(BF)
    for n in (0, 1):
        total = totals[n]
        for s in NEAR:
            slot = lax.rem(z + s, NZ)
            arrived(recv_z.at[n, slot], dz_s.at[n, 0], dz_r.at[n, slot], at_z(s))
            total = total + recv_z[n, slot].astype(F32)
        (lo_ref, ig_ref)[n][...] = unfold(total).astype(BF)
    for c in pending:
        c.wait_send()


def store(a, b, c, d, a_out, b_out, c_out, d_out, sems):
    copies = [
        pltpu.make_async_copy(src, dst, sems.at[i])
        for i, (src, dst) in enumerate(((c, c_out), (d, d_out), (a, a_out), (b, b_out)))
    ]
    for c in copies:
        c.start()
    for c in copies:
        c.wait()


def local(tokens, up_weight, down_weight, cotangent):
    w, h = up_weight.shape
    dma = pltpu.SemaphoreType.DMA
    vmem = pl.BlockSpec(memory_space=pltpu.VMEM)
    hbm = pl.BlockSpec(memory_space=pltpu.HBM)
    shapes = (
        jax.ShapeDtypeStruct((8, w), BF),
        jax.ShapeDtypeStruct((8, w), BF),
        jax.ShapeDtypeStruct((w, h), BF),
        jax.ShapeDtypeStruct((h, w), BF),
    )
    results = pl.pallas_call(
        kernel,
        out_shape=shapes,
        in_specs=[hbm] * 4,
        out_specs=(vmem,) * 4,
        scratch_shapes=[
            pltpu.VMEM((w, h), BF), pltpu.VMEM((h, w), BF),
            pltpu.VMEM((2, 8, w), BF),
            pltpu.VMEM((2, NX, NZ, 16, w // 2), BF),
            pltpu.VMEM((2, 256, w), BF),
            pltpu.VMEM((2, 2, 128, h), F32), pltpu.VMEM((2, 128, h), F32),
            pltpu.VMEM((2, NY, 16, h), BF), pltpu.VMEM((2, NY, 16, h), BF),
            pltpu.VMEM((2, 16, 16, h), BF),
            pltpu.VMEM((2, 256, w), F32),
            pltpu.VMEM((2, NX, NZ, 16, w // 2), BF), pltpu.VMEM((2, NX, NZ, 16, w // 2), BF),
            pltpu.VMEM((2, NZ, 16, w // 2), BF), pltpu.VMEM((2, NZ, 16, w // 2), BF),
            dma((4,)),
            dma((2, NZ)), dma((2, NZ)), dma((2, 4, NX)), dma((2, NX, 4)),
            dma((2,)), dma((2,)),
            dma((2, NY)), dma((2, NY)),
            dma((2, NY)), dma((2, NY)), dma((2, NY)), dma((2, NY)),
            dma((2, 4, NX)), dma((2, NX, 4)), dma((2, NZ)), dma((2, NZ)),
        ],
        compiler_params=pltpu.CompilerParams(
            collective_id=0, has_side_effects=True, vmem_limit_bytes=40 << 20
        ),
        cost_estimate=pl.CostEstimate(flops=1812000000, bytes_accessed=4800000, transcendentals=12288),
        name="sublayer",
    )(*(pltpu.with_memory_space_constraint(a, pltpu.HBM) for a in (tokens, cotangent, up_weight, down_weight)))
    return pl.pallas_call(
        store,
        out_shape=shapes,
        in_specs=[pl.BlockSpec(memory_space=pl.ANY)] * 4,
        out_specs=(hbm,) * 4,
        scratch_shapes=[dma((4,))],
        name="store",
    )(*results)


def solution(mesh):
    in_specs = (P("col", "row"), P("row", "col"), P("col", "row"), P("col", "row"))
    out_specs = (P("col", "row"), P("col", "row"), P("row", "col"), P("col", "row"))
    return jax.shard_map(local, mesh=mesh, in_specs=in_specs, out_specs=out_specs, check_vma=False)
```

time: 423 us -> 140 us (0.33); the launches traced: 418 us -> 140 us
  waiting for transfers between devices: 291 us -> 0 us
  Pallas kernels: 0 us -> 136 us
  blocking collectives: 99.5 us -> 0 us
  between operations: 14.1 us -> 0.65 us
  matrix products: 6.27 us -> 0 us
  other arithmetic: 4.35 us -> 0 us
    reduce_scatter x2 -> x0, waiting for transfers between devices: 291 us -> none  [the longest x1 211 us: local(): results = lax.psum_scatter(products, 'col', scatter_dimension=0, tiled=True)]
    pallas_call x0 -> x2, Pallas kernels: none -> 136 us  [the longest x1 73.3 us: local(): pl.pallas_call(store, out_shape=shapes, in_specs=[pl.BlockSpec(memory_spa...]
    all_gather x3 -> x0, blocking collectives: 99.5 us -> none  [the longest x1 44.5 us: local(): lax.all_gather(tokens, 'col', axis=0, tiled=True)]
    dot_general x6 -> x0, matrix products: 6.27 us -> none  [the longest x2 3.04 us: contract_first(): lax.dot_general(left, right, (((0,), (0,)), ((), ())), preferred_element_...]
  transfers between devices with their start and end apart: 2 -> 0, of which waited for: 2 -> 0; matrix products, arithmetic and copies ran while one was open for 1% -> 0% of each run, Pallas kernels for 0% -> 0%
where the time goes in v2:
time: 140 us
  Pallas kernels  136 us (97%)
  local copies, waits for them, and re-layouts  3.23 us (2%)
    pallas_call x1, Pallas kernels, local(): pl.pallas_call(store, out_shape=shapes, in_specs=[pl.BlockSpec(memory_spa...  73.3 us
    pallas_call x1, Pallas kernels, local(): pl.pallas_call(kernel, out_shape=shapes, in_specs=[hbm] * 4, out_specs=(v...  63.1 us
    unnamed x8, local copies, waits for them, and re-layouts  3.23 us

profile of v2, /device:TPU:1, one launch (start us, length us, event | category | flops | bytes accessed | tf_op | source)
XLA Modules:
  0.0 140.3 jit_solution(16856027859413270738)
XLA Ops:
  0.6 63.1 %sublayer.1 = (bf16[8,768]{1,0:T(8,128)(2,1)S(1)}, bf16[8,768]{1,0:T(8,128)(2,1)S(1)}, bf16[768,768]{1,0:T(8,128)(2,1)S(1)}, bf16[768,768]{1,0:T(8,128)(2,1)S(1)}) custom-call(bf16[8,768]{1,0:T(8,128)(2,1)} %tok_hbm.1, bf16[8,768]{1,0:T(8,128)(2,1)} %cot_hbm.1, bf16[768,768]{1,0:T(8,128)(2,1)} %up_hbm.1, bf16[768,768]{1,0:T(8,128)(2,1)} %down_hbm.1), custom_call_target="tpu_custom_call" | custom-call | flops 1812000000 | bytes 4800000 | tf_op jit(solution)/shard_map/sublayer/pallas_call | solution.py:241
  63.7 0.0 copy-start
  63.7 1.0 copy-done
  64.8 0.0 copy-start.1
  64.8 1.0 copy-done.1
  65.8 0.0 copy-start.2
  65.8 0.6 copy-done.2
  66.4 0.0 copy-start.3
  66.4 0.6 copy-done.3
  67.0 73.3 %store.1 = (bf16[8,768]{1,0:T(8,128)(2,1)}, bf16[8,768]{1,0:T(8,128)(2,1)}, bf16[768,768]{1,0:T(8,128)(2,1)}, bf16[768,768]{1,0:T(8,128)(2,1)}) custom-call(bf16[8,768]{1,0:T(8,128)(2,1)} %copy-done.2, bf16[8,768]{1,0:T(8,128)(2,1)} %copy-done.3, bf16[768,768]{1,0:T(8,128)(2,1)} %copy-done, bf16[768,768]{1,0:T(8,128)(2,1)} %copy-done.1), custom_call_target="tpu_custom_call" | custom-call | tf_op jit(solution)/shard_map/store/pallas_call | solution.py:270
Async XLA Ops:
  63.7 1.0 copy-start
  64.8 1.0 copy-start.1
  65.8 0.6 copy-start.2
  66.4 0.6 copy-start.3

commit v3 on v2

--- a/solution.py
+++ b/solution.py
@@ -273,6 +273,7 @@
         in_specs=[pl.BlockSpec(memory_space=pl.ANY)] * 4,
         out_specs=(hbm,) * 4,
         scratch_shapes=[dma((4,))],
+        compiler_params=pltpu.CompilerParams(vmem_limit_bytes=4 << 20),
         name="store",
     )(*results)
 

time: 140 us -> 65.3 us (0.47)
  Pallas kernels: 136 us -> 64.5 us
  local copies, waits for them, and re-layouts: 3.23 us -> 0 us
    pallas_call x1, Pallas kernels: 73.3 us -> 1.44 us  [local(): pl.pallas_call(store, out_shape=shapes, in_specs=[pl.BlockSpec(memory_spa...]
    unnamed x8 -> x0, local copies, waits for them, and re-layouts: 3.23 us -> none
where the time goes in v3:
time: 65.3 us; the launch traced here: 65.2 us
  Pallas kernels  64.5 us (99%)
    pallas_call x1, Pallas kernels, local(): pl.pallas_call(kernel, out_shape=shapes, in_specs=[hbm] * 4, out_specs=(v...  63.1 us
    pallas_call x1, Pallas kernels, local(): pl.pallas_call(store, out_shape=shapes, in_specs=[pl.BlockSpec(memory_spa...  1.44 us

profile of v3, /device:TPU:1, one launch (start us, length us, event | category | flops | bytes accessed | tf_op | source)
XLA Modules:
  0.0 65.2 jit_solution(17212901299274135713)
XLA Ops:
  0.6 63.1 %sublayer.1 = (bf16[8,768]{1,0:T(8,128)(2,1)S(1)}, bf16[8,768]{1,0:T(8,128)(2,1)S(1)}, bf16[768,768]{1,0:T(8,128)(2,1)S(1)}, bf16[768,768]{1,0:T(8,128)(2,1)S(1)}) custom-call(bf16[8,768]{1,0:T(8,128)(2,1)} %tok_hbm.1, bf16[8,768]{1,0:T(8,128)(2,1)} %cot_hbm.1, bf16[768,768]{1,0:T(8,128)(2,1)} %up_hbm.1, bf16[768,768]{1,0:T(8,128)(2,1)} %down_hbm.1), custom_call_target="tpu_custom_call" | custom-call | flops 1812000000 | bytes 4800000 | tf_op jit(solution)/shard_map/sublayer/pallas_call | solution.py:241
  63.7 1.4 %store.1 = (bf16[8,768]{1,0:T(8,128)(2,1)}, bf16[8,768]{1,0:T(8,128)(2,1)}, bf16[768,768]{1,0:T(8,128)(2,1)}, bf16[768,768]{1,0:T(8,128)(2,1)}) custom-call(bf16[8,768]{1,0:T(8,128)(2,1)S(1)} %get-tuple-element.8.a, bf16[8,768]{1,0:T(8,128)(2,1)S(1)} %get-tuple-element.9.b, bf16[768,768]{1,0:T(8,128)(2,1)S(1)} %get-tuple-element.10.c, ...), custom_call_target="tpu_custom_call" | custom-call | tf_op jit(solution)/shard_map/store/pallas_call | solution.py:270

commit v4 on v3

v4 whole, which is shorter than its diff:
```python
import math

import jax
import jax.numpy as jnp
from jax import lax
from jax.experimental import pallas as pl
from jax.experimental.pallas import tpu as pltpu
from jax.sharding import PartitionSpec as P

coeff_cubic = 0.044715
root_ratio = math.sqrt(2.0 / math.pi)
MESH = pl.DeviceIdType.MESH
BF = jnp.bfloat16
F32 = jnp.float32

NY, NK, NZ, NX = 8, 2, 8, 4
NEAR = (1, 7, 2, 6, 3, 5, 4)
FAR = (4, 3, 5, 2, 6, 1, 7)


def gelu_parts(preact):
    inner = jnp.tanh(root_ratio * (preact + coeff_cubic * preact * preact * preact))
    values = 0.5 * preact * (1.0 + inner)
    slopes = 0.5 * (1.0 + inner) + 0.5 * preact * (1.0 - inner * inner) * root_ratio * (
        1.0 + 3.0 * coeff_cubic * preact * preact
    )
    return (values, slopes)


def dot(left, right, dims):
    return lax.dot_general(left, right, (dims, ((), ())), preferred_element_type=F32)


NN = ((1,), (0,))
NT = ((1,), (1,))
TN = ((0,), (0,))


def fold(block):
    half = block.shape[1] // 2
    return jnp.concatenate([block[:, :half], block[:, half:]], axis=0)


def unfold(block):
    return jnp.concatenate([block[:8], block[8:]], axis=1)


def kernel(
    tok_hbm, cot_hbm, up_hbm, down_hbm,
    lo_ref, ig_ref, ug_ref, dg_ref,
    up, down, shard, gat, xs, part, pair, send_b, recv_b, ah, hid, prod, send_x, recv_x, send_z, recv_z,
    wsem, az_s, ax_s, p_s, b_s, c_s, f_s, dx_s, dz_s,
    az_r, ax_r, p_r, b_r, c_r, f_r, dx_r, dz_r,
):
    row = lax.axis_index("row")
    col = lax.axis_index("col")
    y, k = row // NK, row % NK
    z, x = col // NX, col % NX

    def at_y(d):
        return (lax.rem(y + d, NY) * NK + k, col)

    def at_z(d):
        return (row, lax.rem(z + d, NZ) * NX + x)

    def at_x(d):
        return (row, z * NX + lax.rem(x + d, NX))

    other = (y * NK + 1 - k, col)

    def copy(src, dst, ss, rs, device):
        return pltpu.make_async_remote_copy(
            src_ref=src, dst_ref=dst, send_sem=ss, recv_sem=rs, device_id=device, device_id_type=MESH
        )

    def send(src, dst, ss, rs, device):
        copy(src, dst, ss, rs, device).start()

    def arrived(some, rs):
        copy(some, some, az_s, rs, other).wait_recv()

    load_tok = pltpu.make_async_copy(tok_hbm, shard.at[0], wsem.at[0])
    load_cot = pltpu.make_async_copy(cot_hbm, shard.at[1], wsem.at[1])
    load_up = pltpu.make_async_copy(up_hbm, up, wsem.at[2])
    load_down = pltpu.make_async_copy(down_hbm, down, wsem.at[3])
    load_tok.start()
    load_cot.start()
    load_up.start()
    load_down.start()

    barrier = pltpu.get_barrier_semaphore()
    peers = [at_y(d) for d in FAR] + [at_z(d) for d in FAR] + [at_x(d) for d in (2, 1, 3)] + [other]
    for device in peers:
        pl.semaphore_signal(barrier, inc=1, device_id=device, device_id_type=MESH)
    load_tok.wait()
    load_cot.wait()
    for n in (0, 1):
        gat[n, x, z] = fold(shard[n].astype(F32)).astype(BF)
    pl.semaphore_wait(barrier, len(peers))

    group = z // 4
    half = (1 - group, group)
    near = z // 2
    next_near = near + 1 - 2 * lax.rem(near, 2)
    mate = z + 1 - 2 * lax.rem(z, 2)
    chunks = ((2 * half[0], 2 * half[0] + 1), (next_near, near))

    def send_z_blocks(n):
        for d in FAR:
            send(gat.at[n, x, z], gat.at[n, x, z], az_s, az_r.at[n, near], at_z(d))

    def send_x_blocks(n, t):
        for j in (0, 1) if t == 0 else (1, 0):
            p = chunks[t][j]
            block = gat.at[n, x, pl.ds(2 * p, 2)]
            arrived(gat.at[n, x, mate] if (t, j) == (1, 1) else block, az_r.at[n, p])
            for d in (2, 1, 3):
                send(block, block, ax_s, ax_r.at[n, t], at_x(d))

    def rows_of(t):
        return pl.ds(pl.multiple_of(half[t] * 128, 128), 128)

    mine = pl.ds(pl.multiple_of(k * 64, 64), 64)
    theirs = pl.ds(pl.multiple_of((1 - k) * 64, 64), 64)
    loads = [load_up, load_down]

    def first_product(n, t):
        arrived(gat.at[n, pl.ds(0, 3), pl.ds(0, 4)], ax_r.at[n, t])
        blocks = [unfold(gat[n, j, half[t] * 4 + i].astype(F32)) for i in range(4) for j in range(NX)]
        block = jnp.concatenate(blocks, axis=0).astype(BF)
        xs[n, rows_of(t), :] = block
        if t == 0:
            loads[n].wait()
        weight, dims = ((up, NN), (down, NT))[n]
        c = 2 * n + t
        part[c] = dot(block, weight[...], dims)
        send(part.at[c, theirs], pair.at[c], p_s, p_r.at[c], other)

    own = pl.ds(pl.multiple_of(k * 64 + y * 8, 8), 8)

    def spread(n, t):
        c = 2 * n + t
        arrived(pair.at[c], p_r.at[c])
        for d in FAR + (0,):
            to = lax.rem(y + d, NY)
            rows = pl.ds(pl.multiple_of(k * 64 + to * 8, 8), 8)
            total = part[c, rows, :] + pair[c, pl.ds(pl.multiple_of(to * 8, 8), 8), :]
            if d:
                send_b[c, to] = fold(total).astype(BF)
                send(send_b.at[c, to], recv_b.at[c, y], b_s, b_r.at[c], at_y(d))
            else:
                part[c, rows, :] = total

    at = k * NY + y
    kept = [None, None]

    def middle(n, t):
        c = 2 * n + t
        total = fold(part[c, own, :])
        arrived(recv_b.at[c, pl.ds(0, NY - 1)], b_r.at[c])
        for s in NEAR:
            total = total + recv_b[c, lax.rem(y + s, NY)].astype(F32)
        if n == 0:
            values, kept[t] = gelu_parts(total)
            ah[c, at] = values.astype(BF)
        else:
            ah[c, at] = (total * kept[t]).astype(BF)
        for d in FAR:
            send(ah.at[c, at], ah.at[c, at], c_s, c_r.at[c], at_y(d))

    def forward(n, t):
        c = 2 * n + t
        arrived(ah.at[c, pl.ds(0, NY - 1)], c_r.at[c])
        block = ah.at[c, pl.ds(pl.multiple_of(k * NY, NY), NY)]
        send(block, block, f_s, f_r.at[c], other)

    def second_product(n, t):
        c = 2 * n + t
        arrived(ah.at[c, pl.ds(0, NY)], f_r.at[c])
        block = jnp.concatenate([unfold(ah[c, i].astype(F32)) for i in range(16)], axis=0).astype(BF)
        hid[n, rows_of(t), :] = block
        weight, dims = ((down, NN), (up, NT))[n]
        prod[c] = dot(block, weight[...], dims)
        for j in (0, 1):
            p = chunks[t][j]
            for e in (2, 1, 3):
                to = lax.rem(x + e, NX)
                for i in (0, 1):
                    rows = pl.ds(pl.multiple_of((p - 2 * half[t]) * 64 + i * 32 + to * 8, 8), 8)
                    send_x[n, to, 2 * p + i] = fold(prod[c, rows, :]).astype(BF)
                send(
                    send_x.at[n, to, pl.ds(2 * p, 2)], recv_x.at[n, x, pl.ds(2 * p, 2)],
                    dx_s, dx_r.at[n, p], at_x(e),
                )

    def combine(n, t):
        c = 2 * n + t
        for j in (0, 1):
            p = chunks[t][j]
            arrived(recv_x.at[n, pl.ds(0, 3), pl.ds(0, 2)], dx_r.at[n, p])
            for i in (0, 1):
                last = (t, j) == (1, 1)
                zz = (mate, z)[i] if last else 2 * p + i
                rows = pl.ds(pl.multiple_of((zz - 4 * half[t]) * 32 + x * 8, 8), 8)
                total = fold(prod[c, rows, :])
                for e in (1, 3, 2):
                    total = total + recv_x[n, lax.rem(x + e, NX), zz].astype(F32)
                if not (last and i):
                    send_z[n, zz] = total.astype(BF)
                    send(send_z.at[n, zz], recv_z.at[n, z], dz_s, dz_r.at[n], (row, zz * NX + x))
        return total

    def finish(n, total):
        arrived(recv_z.at[n, pl.ds(0, NZ - 1)], dz_r.at[n])
        for s in NEAR:
            total = total + recv_z[n, lax.rem(z + s, NZ)].astype(F32)
        (lo_ref, ig_ref)[n][...] = unfold(total).astype(BF)

    send_z_blocks(0)
    send_z_blocks(1)
    send_x_blocks(0, 0)
    send_x_blocks(0, 1)
    first_product(0, 0)
    send_x_blocks(1, 0)
    send_x_blocks(1, 1)
    spread(0, 0)
    first_product(0, 1)
    spread(0, 1)
    first_product(1, 0)
    spread(1, 0)
    first_product(1, 1)
    spread(1, 1)
    middle(0, 0)
    middle(0, 1)
    middle(1, 0)
    middle(1, 1)
    forward(0, 0)
    forward(0, 1)
    second_product(0, 0)
    forward(1, 0)
    second_product(0, 1)
    forward(1, 1)
    second_product(1, 0)
    second_product(1, 1)
    combine(0, 0)
    total = combine(0, 1)
    ug_ref[...] = dot(xs[0], hid[1], TN).astype(BF)
    dg_ref[...] = dot(hid[0], xs[1], TN).astype(BF)
    combine(1, 0)
    finish(0, total)
    total = combine(1, 1)
    finish(1, total)
    for sent, sem in (
        (gat.at[:, 0, pl.ds(0, 7)], az_s), (gat.at[:, pl.ds(0, 3)], ax_s), (pair, p_s),
        (send_b.at[:, pl.ds(0, 7)], b_s), (ah.at[:, pl.ds(0, 7)], c_s), (ah.at[:, pl.ds(0, 8)], f_s),
        (send_x.at[:, pl.ds(0, 3)], dx_s), (send_z.at[:, pl.ds(0, 7)], dz_s),
    ):
        copy(sent, sent, sem, dz_r.at[0], other).wait_send()


def store(a, b, c, d, a_out, b_out, c_out, d_out, sems):
    copies = [
        pltpu.make_async_copy(src, dst, sems.at[i])
        for i, (src, dst) in enumerate(((c, c_out), (d, d_out), (a, a_out), (b, b_out)))
    ]
    for c in copies:
        c.start()
    for c in copies:
        c.wait()


def local(tokens, up_weight, down_weight, cotangent):
    w, h = up_weight.shape
    dma = pltpu.SemaphoreType.DMA
    vmem = pl.BlockSpec(memory_space=pltpu.VMEM)
    hbm = pl.BlockSpec(memory_space=pltpu.HBM)
    shapes = (
        jax.ShapeDtypeStruct((8, w), BF),
        jax.ShapeDtypeStruct((8, w), BF),
        jax.ShapeDtypeStruct((w, h), BF),
        jax.ShapeDtypeStruct((h, w), BF),
    )
    results = pl.pallas_call(
        kernel,
        out_shape=shapes,
        in_specs=[hbm] * 4,
        out_specs=(vmem,) * 4,
        scratch_shapes=[
            pltpu.VMEM((w, h), BF), pltpu.VMEM((h, w), BF),
            pltpu.VMEM((2, 8, w), BF),
            pltpu.VMEM((2, NX, NZ, 16, w // 2), BF),
            pltpu.VMEM((2, 256, w), BF),
            pltpu.VMEM((4, 128, h), F32), pltpu.VMEM((4, 64, h), F32),
            pltpu.VMEM((4, NY, 16, h // 2), BF), pltpu.VMEM((4, NY, 16, h // 2), BF),
            pltpu.VMEM((4, 16, 16, h // 2), BF),
            pltpu.VMEM((2, 256, h), BF),
            pltpu.VMEM((4, 128, w), F32),
            pltpu.VMEM((2, NX, NZ, 16, w // 2), BF), pltpu.VMEM((2, NX, NZ, 16, w // 2), BF),
            pltpu.VMEM((2, NZ, 16, w // 2), BF), pltpu.VMEM((2, NZ, 16, w // 2), BF),
            dma((4,)),
            dma, dma, dma, dma, dma, dma, dma, dma,
            dma((2, 4)), dma((2, 2)), dma((4,)), dma((4,)), dma((4,)), dma((4,)), dma((2, 4)), dma((2,)),
        ],
        compiler_params=pltpu.CompilerParams(
            collective_id=0, has_side_effects=True, vmem_limit_bytes=40 << 20
        ),
        cost_estimate=pl.CostEstimate(flops=1812000000, bytes_accessed=4800000, transcendentals=12288),
        name="sublayer",
    )(*(pltpu.with_memory_space_constraint(a, pltpu.HBM) for a in (tokens, cotangent, up_weight, down_weight)))
    return pl.pallas_call(
        store,
        out_shape=shapes,
        in_specs=[pl.BlockSpec(memory_space=pl.ANY)] * 4,
        out_specs=(hbm,) * 4,
        scratch_shapes=[dma((4,))],
        compiler_params=pltpu.CompilerParams(vmem_limit_bytes=4 << 20),
        name="store",
    )(*results)


def solution(mesh):
    in_specs = (P("col", "row"), P("row", "col"), P("col", "row"), P("col", "row"))
    out_specs = (P("col", "row"), P("col", "row"), P("row", "col"), P("col", "row"))
    return jax.shard_map(local, mesh=mesh, in_specs=in_specs, out_specs=out_specs, check_vma=False)
```

time: 65.3 us -> 59.6 us (0.913)
  Pallas kernels: 64.5 us -> 58.8 us
    pallas_call x1, Pallas kernels: 63.1 us -> 57.3 us  [local(): pl.pallas_call(kernel, out_shape=shapes, in_specs=[hbm] * 4, out_specs=(v...]
where the time goes in v4:
time: 59.6 us; the launch traced here: 59.4 us
  Pallas kernels  58.8 us (99%)
  between operations  0.64 us (1%)
    pallas_call x1, Pallas kernels, local(): pl.pallas_call(kernel, out_shape=shapes, in_specs=[hbm] * 4, out_specs=(v...  57.3 us
    pallas_call x1, Pallas kernels, local(): pl.pallas_call(store, out_shape=shapes, in_specs=[pl.BlockSpec(memory_spa...  1.44 us

profile of v4, /device:TPU:1, one launch (start us, length us, event | category | flops | bytes accessed | tf_op | source)
XLA Modules:
  0.0 59.4 jit_solution(17106604446455361800)
XLA Ops:
  0.6 57.3 %sublayer.1 = (bf16[8,768]{1,0:T(8,128)(2,1)S(1)}, bf16[8,768]{1,0:T(8,128)(2,1)S(1)}, bf16[768,768]{1,0:T(8,128)(2,1)S(1)}, bf16[768,768]{1,0:T(8,128)(2,1)S(1)}) custom-call(bf16[8,768]{1,0:T(8,128)(2,1)} %tok_hbm.1, bf16[8,768]{1,0:T(8,128)(2,1)} %cot_hbm.1, bf16[768,768]{1,0:T(8,128)(2,1)} %up_hbm.1, bf16[768,768]{1,0:T(8,128)(2,1)} %down_hbm.1), custom_call_target="tpu_custom_call" | custom-call | flops 1812000000 | bytes 4800000 | tf_op jit(solution)/shard_map/sublayer/pallas_call | solution.py:283
  58.0 1.4 %store.1 = (bf16[8,768]{1,0:T(8,128)(2,1)}, bf16[8,768]{1,0:T(8,128)(2,1)}, bf16[768,768]{1,0:T(8,128)(2,1)}, bf16[768,768]{1,0:T(8,128)(2,1)}) custom-call(bf16[8,768]{1,0:T(8,128)(2,1)S(1)} %get-tuple-element.8.a, bf16[8,768]{1,0:T(8,128)(2,1)S(1)} %get-tuple-element.9.b, bf16[768,768]{1,0:T(8,128)(2,1)S(1)} %get-tuple-element.10.c, ...), custom_call_target="tpu_custom_call" | custom-call | tf_op jit(solution)/shard_map/store/pallas_call | solution.py:310

commit v5 on v4

--- a/solution.py
+++ b/solution.py
@@ -49,8 +49,8 @@
     tok_hbm, cot_hbm, up_hbm, down_hbm,
     lo_ref, ig_ref, ug_ref, dg_ref,
     up, down, shard, gat, xs, part, pair, send_b, recv_b, ah, hid, prod, send_x, recv_x, send_z, recv_z,
-    wsem, az_s, ax_s, p_s, b_s, c_s, f_s, dx_s, dz_s,
-    az_r, ax_r, p_r, b_r, c_r, f_r, dx_r, dz_r,
+    wsem, az_s, ax_s, ao_s, p_s, b_s, c_s, f_s, dx_s, dz_s,
+    az_r, ax_r, ao_r, aw_r, p_r, b_r, c_r, f_r, dx_r, dz_r,
 ):
     row = lax.axis_index("row")
     col = lax.axis_index("col")
@@ -105,16 +105,29 @@
     mate = z + 1 - 2 * lax.rem(z, 2)
     chunks = ((2 * half[0], 2 * half[0] + 1), (next_near, near))
 
+    across = lax.rem(x + 2, NX)
+    sides = ((1, 3), (1, 3))
+
     def send_z_blocks(n):
         for d in FAR:
             send(gat.at[n, x, z], gat.at[n, x, z], az_s, az_r.at[n, near], at_z(d))
+
+    def send_across(n):
+        send(gat.at[n, x, z], gat.at[n, x, z], ao_s, ao_r.at[n], at_x(2))
+
+    def send_far_blocks(n):
+        block = gat.at[n, across, z]
+        arrived(block, ao_r.at[n])
+        for d in FAR:
+            same = lax.rem(lax.rem(z + d, NZ) // 4 + group + 1, 2)
+            send(block, block, az_s, aw_r.at[n, same], at_z(d))
 
     def send_x_blocks(n, t):
         for j in (0, 1) if t == 0 else (1, 0):
             p = chunks[t][j]
             block = gat.at[n, x, pl.ds(2 * p, 2)]
             arrived(gat.at[n, x, mate] if (t, j) == (1, 1) else block, az_r.at[n, p])
-            for d in (2, 1, 3):
+            for d in sides[n]:
                 send(block, block, ax_s, ax_r.at[n, t], at_x(d))
 
     def rows_of(t):
@@ -125,7 +138,9 @@
     loads = [load_up, load_down]
 
     def first_product(n, t):
-        arrived(gat.at[n, pl.ds(0, 3), pl.ds(0, 4)], ax_r.at[n, t])
+        arrived(gat.at[n, pl.ds(0, len(sides[n])), pl.ds(0, 4)], ax_r.at[n, t])
+        if len(sides[n]) == 2:
+            arrived(gat.at[n, 0, pl.ds(0, 4 - t)], aw_r.at[n, t])
         blocks = [unfold(gat[n, j, half[t] * 4 + i].astype(F32)) for i in range(4) for j in range(NX)]
         block = jnp.concatenate(blocks, axis=0).astype(BF)
         xs[n, rows_of(t), :] = block
@@ -216,13 +231,17 @@
             total = total + recv_z[n, lax.rem(z + s, NZ)].astype(F32)
         (lo_ref, ig_ref)[n][...] = unfold(total).astype(BF)
 
+    send_across(0)
     send_z_blocks(0)
+    send_across(1)
     send_z_blocks(1)
+    send_far_blocks(0)
     send_x_blocks(0, 0)
     send_x_blocks(0, 1)
-    first_product(0, 0)
+    send_far_blocks(1)
     send_x_blocks(1, 0)
     send_x_blocks(1, 1)
+    first_product(0, 0)
     spread(0, 0)
     first_product(0, 1)
     spread(0, 1)
@@ -237,21 +256,22 @@
     forward(0, 0)
     forward(0, 1)
     second_product(0, 0)
+    second_product(0, 1)
     forward(1, 0)
-    second_product(0, 1)
     forward(1, 1)
     second_product(1, 0)
     second_product(1, 1)
     combine(0, 0)
-    total = combine(0, 1)
+    last01 = combine(0, 1)
+    combine(1, 0)
     ug_ref[...] = dot(xs[0], hid[1], TN).astype(BF)
     dg_ref[...] = dot(hid[0], xs[1], TN).astype(BF)
-    combine(1, 0)
-    finish(0, total)
-    total = combine(1, 1)
-    finish(1, total)
+    finish(0, last01)
+    last11 = combine(1, 1)
+    finish(1, last11)
     for sent, sem in (
-        (gat.at[:, 0, pl.ds(0, 7)], az_s), (gat.at[:, pl.ds(0, 3)], ax_s), (pair, p_s),
+        (gat.at[:, pl.ds(0, 2), pl.ds(0, 7)], az_s), (gat.at[:, pl.ds(0, 2)], ax_s),
+        (gat.at[0, 0, pl.ds(0, 2)], ao_s), (pair, p_s),
         (send_b.at[:, pl.ds(0, 7)], b_s), (ah.at[:, pl.ds(0, 7)], c_s), (ah.at[:, pl.ds(0, 8)], f_s),
         (send_x.at[:, pl.ds(0, 3)], dx_s), (send_z.at[:, pl.ds(0, 7)], dz_s),
     ):
@@ -298,8 +318,8 @@
             pltpu.VMEM((2, NX, NZ, 16, w // 2), BF), pltpu.VMEM((2, NX, NZ, 16, w // 2), BF),
             pltpu.VMEM((2, NZ, 16, w // 2), BF), pltpu.VMEM((2, NZ, 16, w // 2), BF),
             dma((4,)),
-            dma, dma, dma, dma, dma, dma, dma, dma,
-            dma((2, 4)), dma((2, 2)), dma((4,)), dma((4,)), dma((4,)), dma((4,)), dma((2, 4)), dma((2,)),
+            dma, dma, dma, dma, dma, dma, dma, dma, dma,
+            dma((2, 4)), dma((2, 2)), dma((2,)), dma((2, 2)), dma((4,)), dma((4,)), dma((4,)), dma((4,)), dma((2, 4)), dma((2,)),
         ],
         compiler_params=pltpu.CompilerParams(
             collective_id=0, has_side_effects=True, vmem_limit_bytes=40 << 20

time: 59.6 us -> 58.3 us (0.978)
  Pallas kernels: 58.8 us -> 57.5 us
    pallas_call x1, Pallas kernels: 57.3 us -> 56 us  [local(): pl.pallas_call(kernel, out_shape=shapes, in_specs=[hbm] * 4, out_specs=(v...]
where the time goes in v5:
time: 58.3 us; the launch traced here: 58.1 us
  Pallas kernels  57.5 us (99%)
  between operations  0.64 us (1%)
    pallas_call x1, Pallas kernels, local(): pl.pallas_call(kernel, out_shape=shapes, in_specs=[hbm] * 4, out_specs=(v...  56 us
    pallas_call x1, Pallas kernels, local(): pl.pallas_call(store, out_shape=shapes, in_specs=[pl.BlockSpec(memory_spa...  1.44 us

profile of v5, /device:TPU:1, one launch (start us, length us, event | category | flops | bytes accessed | tf_op | source)
XLA Modules:
  0.0 58.1 jit_solution(13508607893421478691)
XLA Ops:
  0.6 56.0 %sublayer.1 = (bf16[8,768]{1,0:T(8,128)(2,1)S(1)}, bf16[8,768]{1,0:T(8,128)(2,1)S(1)}, bf16[768,768]{1,0:T(8,128)(2,1)S(1)}, bf16[768,768]{1,0:T(8,128)(2,1)S(1)}) custom-call(bf16[8,768]{1,0:T(8,128)(2,1)} %tok_hbm.1, bf16[8,768]{1,0:T(8,128)(2,1)} %cot_hbm.1, bf16[768,768]{1,0:T(8,128)(2,1)} %up_hbm.1, bf16[768,768]{1,0:T(8,128)(2,1)} %down_hbm.1), custom_call_target="tpu_custom_call" | custom-call | flops 1812000000 | bytes 4800000 | tf_op jit(solution)/shard_map/sublayer/pallas_call | solution.py:303
  56.7 1.4 %store.1 = (bf16[8,768]{1,0:T(8,128)(2,1)}, bf16[8,768]{1,0:T(8,128)(2,1)}, bf16[768,768]{1,0:T(8,128)(2,1)}, bf16[768,768]{1,0:T(8,128)(2,1)}) custom-call(bf16[8,768]{1,0:T(8,128)(2,1)S(1)} %get-tuple-element.8.a, bf16[8,768]{1,0:T(8,128)(2,1)S(1)} %get-tuple-element.9.b, bf16[768,768]{1,0:T(8,128)(2,1)S(1)} %get-tuple-element.10.c, ...), custom_call_target="tpu_custom_call" | custom-call | tf_op jit(solution)/shard_map/store/pallas_call | solution.py:330

commit v6 on v5

--- a/solution.py
+++ b/solution.py
@@ -79,6 +79,10 @@
     def arrived(some, rs):
         copy(some, some, az_s, rs, other).wait_recv()
 
+    barrier = pltpu.get_barrier_semaphore()
+    peers = [at_y(d) for d in FAR] + [at_z(d) for d in FAR] + [at_x(d) for d in (2, 1, 3)] + [other]
+    for device in peers:
+        pl.semaphore_signal(barrier, inc=1, device_id=device, device_id_type=MESH)
     load_tok = pltpu.make_async_copy(tok_hbm, shard.at[0], wsem.at[0])
     load_cot = pltpu.make_async_copy(cot_hbm, shard.at[1], wsem.at[1])
     load_up = pltpu.make_async_copy(up_hbm, up, wsem.at[2])
@@ -88,10 +92,6 @@
     load_up.start()
     load_down.start()
 
-    barrier = pltpu.get_barrier_semaphore()
-    peers = [at_y(d) for d in FAR] + [at_z(d) for d in FAR] + [at_x(d) for d in (2, 1, 3)] + [other]
-    for device in peers:
-        pl.semaphore_signal(barrier, inc=1, device_id=device, device_id_type=MESH)
     load_tok.wait()
     load_cot.wait()
     for n in (0, 1):
@@ -254,20 +254,20 @@
     middle(1, 0)
     middle(1, 1)
     forward(0, 0)
+    second_product(0, 0)
     forward(0, 1)
-    second_product(0, 0)
     second_product(0, 1)
     forward(1, 0)
+    second_product(1, 0)
     forward(1, 1)
-    second_product(1, 0)
     second_product(1, 1)
     combine(0, 0)
     last01 = combine(0, 1)
     combine(1, 0)
+    last11 = combine(1, 1)
     ug_ref[...] = dot(xs[0], hid[1], TN).astype(BF)
     dg_ref[...] = dot(hid[0], xs[1], TN).astype(BF)
     finish(0, last01)
-    last11 = combine(1, 1)
     finish(1, last11)
     for sent, sem in (
         (gat.at[:, pl.ds(0, 2), pl.ds(0, 7)], az_s), (gat.at[:, pl.ds(0, 2)], ax_s),

time: 58.3 us -> 57.2 us (0.981)
  Pallas kernels: 57.5 us -> 56.4 us
    pallas_call x1, Pallas kernels: 56 us -> 54.9 us  [local(): pl.pallas_call(kernel, out_shape=shapes, in_specs=[hbm] * 4, out_specs=(v...]
where the time goes in v6:
time: 57.2 us; the launch traced here: 57 us
  Pallas kernels  56.4 us (99%)
  between operations  0.64 us (1%)
    pallas_call x1, Pallas kernels, local(): pl.pallas_call(kernel, out_shape=shapes, in_specs=[hbm] * 4, out_specs=(v...  54.9 us
    pallas_call x1, Pallas kernels, local(): pl.pallas_call(store, out_shape=shapes, in_specs=[pl.BlockSpec(memory_spa...  1.44 us

profile of v6, /device:TPU:1, one launch (start us, length us, event | category | flops | bytes accessed | tf_op | source)
XLA Modules:
  0.0 57.0 jit_solution(5707498879082100057)
XLA Ops:
  0.6 54.9 %sublayer.1 = (bf16[8,768]{1,0:T(8,128)(2,1)S(1)}, bf16[8,768]{1,0:T(8,128)(2,1)S(1)}, bf16[768,768]{1,0:T(8,128)(2,1)S(1)}, bf16[768,768]{1,0:T(8,128)(2,1)S(1)}) custom-call(bf16[8,768]{1,0:T(8,128)(2,1)} %tok_hbm.1, bf16[8,768]{1,0:T(8,128)(2,1)} %cot_hbm.1, bf16[768,768]{1,0:T(8,128)(2,1)} %up_hbm.1, bf16[768,768]{1,0:T(8,128)(2,1)} %down_hbm.1), custom_call_target="tpu_custom_call" | custom-call | flops 1812000000 | bytes 4800000 | tf_op jit(solution)/shard_map/sublayer/pallas_call | solution.py:303
  55.6 1.4 %store.1 = (bf16[8,768]{1,0:T(8,128)(2,1)}, bf16[8,768]{1,0:T(8,128)(2,1)}, bf16[768,768]{1,0:T(8,128)(2,1)}, bf16[768,768]{1,0:T(8,128)(2,1)}) custom-call(bf16[8,768]{1,0:T(8,128)(2,1)S(1)} %get-tuple-element.8.a, bf16[8,768]{1,0:T(8,128)(2,1)S(1)} %get-tuple-element.9.b, bf16[768,768]{1,0:T(8,128)(2,1)S(1)} %get-tuple-element.10.c, ...), custom_call_target="tpu_custom_call" | custom-call | tf_op jit(solution)/shard_map/store/pallas_call | solution.py:330
